TPU v7x, 32 devices: a whole 2x2x4 slice. The times are simulated.
32 devices in a mesh: sky: 16 (over z, x, core), exp: 2 (over y).
Axes of the slice: x: 2, y: 2, z: 4, core: 2. Of those that a mesh axis runs over, the one named last changes fastest.
Arguments:
- padded_tiles: bfloat16 [1536, 10752], P(('sky', 'exp')), may hold values from -6 to 6
- coefficients: float32 [1536, 20], P(('sky', 'exp')), may hold values from -1.8 to 1.8
- row_taps: bfloat16 [1536, 6, 24], P(('sky', 'exp')), may hold values from 0.019897461 to 0.34960938
- col_taps: bfloat16 [1536, 6, 128], P(('sky', 'exp')), may hold values from 0.019897461 to 0.34960938
- shifts: int32 [1536, 2], P(('sky', 'exp')), may hold values from 0 to 2
- mask_words: int32 [1536], P(('sky', 'exp')), may hold values from -2147483648 to 2147483646
- weights: bfloat16 [1536], P(('sky', 'exp')), may hold values from 0.049804688 to 0.5
- destination: int32 [1536, 1], P(('sky', 'exp')), may hold values from 0 to 15; in each aligned block of 48 rows (0 to 47, 48 to 95, ...) at most 6 rows name the same one
- patch_slot: int32 [1536], P(('sky', 'exp')), may hold values from 0 to 15
- basis_rows: bfloat16 [20, 41], replicated, may hold values from -1 to 1
- basis_cols: bfloat16 [20, 41], replicated, may hold values from -1 to 1
Outputs:
- coadd: float32 [6144, 128], P(('sky', 'exp'))
Inputs may be any that keep to these rules, and one draw needn't show every extreme that they name: `destination`: the 48 tiles of one device name one patch at most 6 times, a bound that some block reaches.
All inputs are finite; a program needn't handle non-finite values.
Results may differ from a plain program's by a relative error of at most 0.014.
Values may be sent and summed in bfloat16 or wider, within the bound.
A program may use at most 64 MiB of HBM per device.

v0:
```python
import jax
import jax.numpy as jnp
from jax import lax
from jax.sharding import PartitionSpec as P

SLOTS = 16


def toeplitz(basis_vals, distance):
    kernel_len = basis_vals.shape[1]
    picks = (distance[:, :, None] == jnp.arange(kernel_len, dtype=jnp.int32)[None, None, :]).astype(
        jnp.float32
    )
    return jnp.einsum("xyk,bk->bxy", picks, basis_vals.astype(jnp.float32)).astype(jnp.bfloat16)


def build_tables(basis_rows, basis_cols, tile_rows, tile_cols):
    kernel_len = basis_rows.shape[1]
    out_rows = jnp.arange(tile_rows, dtype=jnp.int32)
    in_rows = jnp.arange(tile_rows + kernel_len - 1, dtype=jnp.int32)
    out_cols = jnp.arange(tile_cols, dtype=jnp.int32)
    in_cols = jnp.arange(tile_cols + kernel_len - 1, dtype=jnp.int32)
    row_toeplitz = toeplitz(basis_rows, in_rows[None, :] - out_rows[:, None])
    col_toeplitz = toeplitz(basis_cols, in_cols[:, None] - out_cols[None, :])
    return (row_toeplitz, col_toeplitz)


def band_matrix(tap_values, band_shift):
    tap_count = tap_values.shape[1]
    length = tap_values.shape[2]
    positions = jnp.arange(length, dtype=jnp.int32)
    band_start = jnp.clip(
        positions[None, :] + band_shift[:, None] - tap_count // 2, 0, length - tap_count
    )
    band_offset = positions[None, None, :] - band_start[:, :, None]
    matrix = jnp.zeros((tap_values.shape[0], length, length), tap_values.dtype)
    for tap_index in range(tap_count):
        matrix = matrix + jnp.where(
            band_offset == tap_index,
            tap_values[:, tap_index, :][:, :, None],
            jnp.zeros((), tap_values.dtype),
        )
    return matrix


def mask_good(mask_words, tile_rows, tile_cols):
    bit_index = jnp.arange(32, dtype=jnp.int32)
    flagged = jnp.bitwise_and(jnp.right_shift(mask_words[:, None], bit_index[None, :]), 1)
    good_cells = (1 - flagged).astype(jnp.float32).reshape(mask_words.shape[0], 4, 8)
    good_cells = jnp.repeat(good_cells, tile_rows // 4, axis=1)
    return jnp.repeat(good_cells, tile_cols // 8, axis=2)


def body(
    padded_tiles,
    coefficients,
    row_taps,
    col_taps,
    shifts,
    mask_words,
    weights,
    destination,
    patch_slot,
    basis_rows,
    basis_cols,
):
    sky_count = lax.axis_size("sky")
    tiles_dev = padded_tiles.shape[0]
    tile_rows = row_taps.shape[2]
    tile_cols = col_taps.shape[2]
    kernel_len = basis_rows.shape[1]
    slot_count = SLOTS
    capacity = 2 * ((tiles_dev + sky_count - 1) // sky_count)
    row_toeplitz, col_toeplitz = build_tables(basis_rows, basis_cols, tile_rows, tile_cols)
    per_block = 8
    block_count = tiles_dev // per_block

    def match_and_warp(tile_group):
        padded, coef_block, rtap, ctap, shift_block = tile_group
        padded = padded.reshape(per_block, tile_rows + kernel_len - 1, tile_cols + kernel_len - 1)
        row_pass = jnp.einsum(
            "bic,ncj->nbij", row_toeplitz, padded, preferred_element_type=jnp.float32
        )
        scaled = (row_pass * coef_block[:, :, None, None]).astype(jnp.bfloat16)
        matched = jnp.einsum(
            "nbij,bjk->nik", scaled, col_toeplitz, preferred_element_type=jnp.float32
        ).astype(jnp.bfloat16)
        row_warp = band_matrix(rtap, shift_block[:, 0])
        col_warp = band_matrix(ctap, shift_block[:, 1])
        halfway = jnp.einsum(
            "nij,njk->nik", row_warp, matched, preferred_element_type=jnp.float32
        ).astype(jnp.bfloat16)
        return jnp.einsum(
            "nij,nkj->nik", halfway, col_warp, preferred_element_type=jnp.float32
        ).astype(jnp.bfloat16)

    inputs = (padded_tiles, coefficients, row_taps, col_taps, shifts)
    grouped = tuple((arr.reshape((block_count, per_block) + arr.shape[1:]) for arr in inputs))
    warped = lax.map(match_and_warp, grouped).reshape(tiles_dev, tile_rows * tile_cols)
    dest_flat = destination[:, 0]
    dest_onehot = (dest_flat[:, None] == jnp.arange(sky_count, dtype=jnp.int32)[None, :]).astype(
        jnp.int32
    )
    before = jnp.cumsum(dest_onehot, axis=0) - dest_onehot
    dest_rank = jnp.sum(before * dest_onehot, axis=1)
    target = dest_flat * capacity + dest_rank
    chosen = jnp.arange(sky_count * capacity, dtype=jnp.int32)[:, None] == target[None, :]
    select = chosen.astype(jnp.bfloat16)
    slot_onehot = (patch_slot[:, None] == jnp.arange(slot_count, dtype=jnp.int32)[None, :]).astype(
        jnp.bfloat16
    )
    send_tiles = jnp.dot(select, warped, preferred_element_type=jnp.float32).astype(jnp.bfloat16)
    good_cells = mask_good(mask_words, tile_rows, tile_cols)
    weight_plane = (
        (weights.astype(jnp.float32)[:, None, None] * good_cells)
        .astype(jnp.bfloat16)
        .reshape(tiles_dev, tile_rows * tile_cols)
    )
    send_planes = jnp.dot(select, weight_plane, preferred_element_type=jnp.float32).astype(
        jnp.bfloat16
    )
    send_slots = jnp.dot(select, slot_onehot, preferred_element_type=jnp.float32).astype(
        jnp.bfloat16
    )
    recv_tiles, recv_planes, recv_slots = (
        lax.all_to_all(send_tiles, "sky", split_axis=0, concat_axis=0, tiled=True),
        lax.all_to_all(send_planes, "sky", split_axis=0, concat_axis=0, tiled=True),
        lax.all_to_all(send_slots, "sky", split_axis=0, concat_axis=0, tiled=True),
    )
    plane_vals = recv_planes.astype(jnp.float32)
    products = plane_vals * recv_tiles.astype(jnp.float32)
    slot_vals = recv_slots.astype(jnp.float32).T
    numerator = jnp.dot(slot_vals, products, precision=lax.Precision.HIGHEST)
    weight_sum = jnp.dot(slot_vals, plane_vals, precision=lax.Precision.HIGHEST)
    numerator = numerator.reshape(slot_count * tile_rows, tile_cols)
    weight_sum = weight_sum.reshape(slot_count * tile_rows, tile_cols)
    totals = (
        lax.psum_scatter(
            numerator.astype(jnp.bfloat16), "exp", scatter_dimension=0, tiled=True
        ).astype(jnp.float32),
        lax.psum_scatter(
            weight_sum.astype(jnp.bfloat16), "exp", scatter_dimension=0, tiled=True
        ).astype(jnp.float32),
    )
    return totals[0] / jnp.maximum(totals[1], 1.0)


def solution(mesh):
    placed = (
        P(("sky", "exp"), None),
        P(("sky", "exp"), None),
        P(("sky", "exp"), None, None),
        P(("sky", "exp"), None, None),
        P(("sky", "exp"), None),
        P(("sky", "exp")),
        P(("sky", "exp")),
        P(("sky", "exp"), None),
        P(("sky", "exp")),
        P(),
        P(),
    )
    return jax.shard_map(
        body, mesh=mesh, in_specs=placed, out_specs=P(("sky", "exp"), None), check_vma=False
    )
```

profile of v0, /device:TPU:0, one launch (start us, length us, event | category | flops | bytes accessed | tf_op | source)
XLA Modules:
  0.0 119.2 jit_solution(8791408649160191520)
XLA Ops:
  10.5 7.4 %all-to-all-start = ((bf16[16,6,16]{2,1,0:T(8,128)(2,1)}), bf16[16,6,16]{2,1,0:T(8,128)(2,1)S(1)}, u32[]{:S(2)}, u32[]{:S(2)}) async-start(bf16[16,6,16]{2,1,0:T(8,128)(2,1)} %all_to_all.18), calls=%async_computation | async-start | bytes 65536 | tf_op jit(solution)/shard_map/all_to_all | solution.py:128
  21.0 1.1 all_to_all.20
  22.6 2.0 %all-to-all-done = bf16[16,6,16]{2,1,0:T(8,128)(2,1)S(1)} async-done(((bf16[16,6,16]{2,1,0:T(8,128)(2,1)}), bf16[16,6,16]{2,1,0:T(8,128)(2,1)S(1)}, u32[]{:S(2)}, u32[]{:S(2)}) %all-to-all-start) | async-done | bytes 3104 | tf_op jit(solution)/shard_map/all_to_all | solution.py:128
  24.5 4.0 %all-to-all-start.1 = ((bf16[16,6,3072]{2,1,0:T(8,128)(2,1)}), bf16[16,6,3072]{2,1,0:T(8,128)(2,1)S(1)}, u32[]{:S(2)}, u32[]{:S(2)}) async-start(bf16[16,6,3072]{2,1,0:T(8,128)(2,1)} %all_to_all.20), calls=%async_computation.1 | async-start | bytes 1572864 | tf_op jit(solution)/shard_map/all_to_all | solution.py:127
  28.6 30.8 %while.13 = (s32[]{:T(128)}, bf16[6,8,24,128]{3,2,1,0:T(8,128)(2,1)S(1)}, s32[6,8,2]{1,0,2:T(8,128)S(1)}, bf16[6,8,6,24]{3,1,0,2:T(8,128)(2,1)S(1)}, bf16[6,8,10...) while((s32[]{:T(128)}, ...), condition=%wide.region_3.4_spmd, body=%wide.region_2.3_spmd.sunk | while | flops 259956800 | bytes 2027581 | solution.py:99
  30.3 1.1 fusion.163
  32.3 1.4 %fusion.164 = bf16[6,8,24,128]{3,2,1,0:T(8,128)(2,1)S(1)} fusion(bf16[6,8,24,128]{3,2,1,0:T(8,128)(2,1)S(1)} %get-tuple-element.296, s32[]{:T(128)} %get-tuple-element.295, bf16[8,24,128]{2,1,0:T(8,128)(2,1)S(1)} %fusion.163, s32[8,128]{1,0:T(8,128)S(1)} %add_clamp_fusion.4, bf16[8,128]{1,0:T(8,128)(2,1)S(1)} %get-tuple-element.272, ...), kind=kOutput, calls=%fused_computation.8.clone.1 | convolution fusion | flops 10912256 | bytes 131076 | tf_op jit(solution)/shard_map/while/body/eval_jaxpr/nij,nkj->nik/dot_general | solution.py:93
  35.4 1.1 fusion.163
  37.5 1.4 %fusion.164 = bf16[6,8,24,128]{3,2,1,0:T(8,128)(2,1)S(1)} fusion(bf16[6,8,24,128]{3,2,1,0:T(8,128)(2,1)S(1)} %get-tuple-element.296, s32[]{:T(128)} %get-tuple-element.295, bf16[8,24,128]{2,1,0:T(8,128)(2,1)S(1)} %fusion.163, s32[8,128]{1,0:T(8,128)S(1)} %add_clamp_fusion.4, bf16[8,128]{1,0:T(8,128)(2,1)S(1)} %get-tuple-element.272, ...), kind=kOutput, calls=%fused_computation.8.clone.1 | convolution fusion | flops 10912256 | bytes 131076 | tf_op jit(solution)/shard_map/while/body/eval_jaxpr/nij,nkj->nik/dot_general | solution.py:93
  40.6 1.1 fusion.163
  42.6 1.4 %fusion.164 = bf16[6,8,24,128]{3,2,1,0:T(8,128)(2,1)S(1)} fusion(bf16[6,8,24,128]{3,2,1,0:T(8,128)(2,1)S(1)} %get-tuple-element.296, s32[]{:T(128)} %get-tuple-element.295, bf16[8,24,128]{2,1,0:T(8,128)(2,1)S(1)} %fusion.163, s32[8,128]{1,0:T(8,128)S(1)} %add_clamp_fusion.4, bf16[8,128]{1,0:T(8,128)(2,1)S(1)} %get-tuple-element.272, ...), kind=kOutput, calls=%fused_computation.8.clone.1 | convolution fusion | flops 10912256 | bytes 131076 | tf_op jit(solution)/shard_map/while/body/eval_jaxpr/nij,nkj->nik/dot_general | solution.py:93
  45.7 1.1 fusion.163
  47.7 1.4 %fusion.164 = bf16[6,8,24,128]{3,2,1,0:T(8,128)(2,1)S(1)} fusion(bf16[6,8,24,128]{3,2,1,0:T(8,128)(2,1)S(1)} %get-tuple-element.296, s32[]{:T(128)} %get-tuple-element.295, bf16[8,24,128]{2,1,0:T(8,128)(2,1)S(1)} %fusion.163, s32[8,128]{1,0:T(8,128)S(1)} %add_clamp_fusion.4, bf16[8,128]{1,0:T(8,128)(2,1)S(1)} %get-tuple-element.272, ...), kind=kOutput, calls=%fused_computation.8.clone.1 | convolution fusion | flops 10912256 | bytes 131076 | tf_op jit(solution)/shard_map/while/body/eval_jaxpr/nij,nkj->nik/dot_general | solution.py:93
  50.8 1.1 fusion.163
  52.9 1.4 %fusion.164 = bf16[6,8,24,128]{3,2,1,0:T(8,128)(2,1)S(1)} fusion(bf16[6,8,24,128]{3,2,1,0:T(8,128)(2,1)S(1)} %get-tuple-element.296, s32[]{:T(128)} %get-tuple-element.295, bf16[8,24,128]{2,1,0:T(8,128)(2,1)S(1)} %fusion.163, s32[8,128]{1,0:T(8,128)S(1)} %add_clamp_fusion.4, bf16[8,128]{1,0:T(8,128)(2,1)S(1)} %get-tuple-element.272, ...), kind=kOutput, calls=%fused_computation.8.clone.1 | convolution fusion | flops 10912256 | bytes 131076 | tf_op jit(solution)/shard_map/while/body/eval_jaxpr/nij,nkj->nik/dot_general | solution.py:93
  56.0 1.1 fusion.163
  58.0 1.4 %fusion.164 = bf16[6,8,24,128]{3,2,1,0:T(8,128)(2,1)S(1)} fusion(bf16[6,8,24,128]{3,2,1,0:T(8,128)(2,1)S(1)} %get-tuple-element.296, s32[]{:T(128)} %get-tuple-element.295, bf16[8,24,128]{2,1,0:T(8,128)(2,1)S(1)} %fusion.163, s32[8,128]{1,0:T(8,128)S(1)} %add_clamp_fusion.4, bf16[8,128]{1,0:T(8,128)(2,1)S(1)} %get-tuple-element.272, ...), kind=kOutput, calls=%fused_computation.8.clone.1 | convolution fusion | flops 10912256 | bytes 131076 | tf_op jit(solution)/shard_map/while/body/eval_jaxpr/nij,nkj->nik/dot_general | solution.py:93
  59.7 1.1 all_to_all.22
  60.8 6.0 %all-to-all-start.2 = ((bf16[16,6,3072]{2,1,0:T(8,128)(2,1)}), bf16[16,6,3072]{2,1,0:T(8,128)(2,1)S(1)}, u32[]{:S(2)}, u32[]{:S(2)}) async-start(bf16[16,6,3072]{2,1,0:T(8,128)(2,1)} %all_to_all.22), calls=%async_computation.2 | async-start | bytes 1572864 | tf_op jit(solution)/shard_map/all_to_all | solution.py:126
  66.9 18.6 %all-to-all-done.2 = bf16[16,6,3072]{2,1,0:T(8,128)(2,1)S(1)} async-done(((bf16[16,6,3072]{2,1,0:T(8,128)(2,1)}), bf16[16,6,3072]{2,1,0:T(8,128)(2,1)S(1)}, u32[]{:S(2)}, u32[]{:S(2)}) %all-to-all-start.2) | async-done | bytes 589856 | tf_op jit(solution)/shard_map/all_to_all | solution.py:126
  85.7 1.3 %fusion.124 = bf16[16,3072]{1,0:T(8,128)(2,1)S(1)} fusion(bf16[16,6,16]{0,2,1:T(8,128)(2,1)S(1)} %copy.38, f32[16,6,3072]{2,1,0:T(8,128)S(1)} %convert_multiply_fusion), kind=kOutput, calls=%fused_computation.110 | convolution fusion | flops 56672256 | bytes 1281024 | tf_op jit(solution)/shard_map/dot_general | solution.py:133
  88.9 9.8 %reduce-scatter.3.cloned.1.call-done = bf16[192,128]{1,0:T(8,128)(2,1)} async-done(((bf16[384,128]{1,0:T(8,128)(2,1)}), bf16[192,128]{1,0:T(8,128)(2,1)}) %reduce-scatter.3.cloned.1.call-update) | async-done | bytes 49168 | tf_op jit(solution)/shard_map/reduce_scatter | solution.py:138
  98.7 12.2 %reduce-scatter.5.cloned.1.call-done = bf16[192,128]{1,0:T(8,128)(2,1)} async-done(((bf16[384,128]{1,0:T(8,128)(2,1)}), bf16[192,128]{1,0:T(8,128)(2,1)}) %reduce-scatter.5.cloned.1.call-update) | async-done | bytes 49168 | tf_op jit(solution)/shard_map/reduce_scatter | solution.py:141
  110.9 1.5 %maximum_divide_fusion = f32[192,128]{1,0:T(8,128)} fusion(bf16[192,128]{1,0:T(8,128)(2,1)} %reduce-scatter.5.cloned.1.call-done, bf16[192,128]{1,0:T(8,128)(2,1)} %reduce-scatter.3.cloned.1.call-done), kind=kLoop, calls=%fused_computation.127 | loop fusion | flops 98304 | bytes 196608 | tf_op jit(solution)/shard_map/div | solution.py:145
  (110 shorter events, 25.5 us)
Async XLA Ops:
  6.5 13.3 %copy-start = (bf16[20,41]{1,0:T(8,128)(2,1)S(1)}, bf16[20,41]{1,0:T(8,128)(2,1)}, u32[]{:S(2)}) copy-start(bf16[20,41]{1,0:T(8,128)(2,1)} %param.23) | copy-start | bytes 4924
  10.5 14.0 %all-to-all-start = ((bf16[16,6,16]{2,1,0:T(8,128)(2,1)}), bf16[16,6,16]{2,1,0:T(8,128)(2,1)S(1)}, u32[]{:S(2)}, u32[]{:S(2)}) async-start(bf16[16,6,16]{2,1,0:T(8,128)(2,1)} %all_to_all.18), calls=%async_computation | async-start | bytes 65536 | tf_op jit(solution)/shard_map/all_to_all | solution.py:128
  19.3 1.4 %copy-start.4 = (bf16[20,41]{1,0:T(8,128)(2,1)S(1)}, bf16[20,41]{1,0:T(8,128)(2,1)}, u32[]{:S(2)}) copy-start(bf16[20,41]{1,0:T(8,128)(2,1)} %param.22) | copy-start | bytes 4924
  21.0 1.3 %copy-start.1 = (bf16[48,6,24]{0,2,1:T(8,128)(2,1)S(1)}, bf16[48,6,24]{0,2,1:T(8,128)(2,1)}, u32[]{:S(2)}) copy-start(bf16[48,6,24]{0,2,1:T(8,128)(2,1)} %param.15) | copy-start | bytes 41476
  21.0 1.4 %copy-start.2 = (f32[48,20]{0,1:T(8,128)S(1)}, f32[48,20]{0,1:T(8,128)}, u32[]{:S(2)}) copy-start(f32[48,20]{0,1:T(8,128)} %param.14) | copy-start | bytes 11524
  21.0 1.5 %copy-start.3 = (s32[48,2]{0,1:T(2,128)S(1)}, s32[48,2]{0,1:T(2,128)}, u32[]{:S(2)}) copy-start(s32[48,2]{0,1:T(2,128)} %param.17) | copy-start | bytes 1156
  24.5 36.3 %all-to-all-start.1 = ((bf16[16,6,3072]{2,1,0:T(8,128)(2,1)}), bf16[16,6,3072]{2,1,0:T(8,128)(2,1)S(1)}, u32[]{:S(2)}, u32[]{:S(2)}) async-start(bf16[16,6,3072]{2,1,0:T(8,128)(2,1)} %all_to_all.20), calls=%async_computation.1 | async-start | bytes 1572864 | tf_op jit(solution)/shard_map/all_to_all | solution.py:127
  60.8 24.7 %all-to-all-start.2 = ((bf16[16,6,3072]{2,1,0:T(8,128)(2,1)}), bf16[16,6,3072]{2,1,0:T(8,128)(2,1)S(1)}, u32[]{:S(2)}, u32[]{:S(2)}) async-start(bf16[16,6,3072]{2,1,0:T(8,128)(2,1)} %all_to_all.22), calls=%async_computation.2 | async-start | bytes 1572864 | tf_op jit(solution)/shard_map/all_to_all | solution.py:126
  66.8 31.9 %reduce-scatter.3.cloned.1.call-start = ((), (), s32[]{:S(2)}) async-start(), calls=%async_computation.5 | async-start | bytes 147456 | tf_op jit(solution)/shard_map/reduce_scatter | solution.py:138
  87.7 23.2 %reduce-scatter.5.cloned.1.call-start = ((), (), s32[]{:S(2)}) async-start(), calls=%async_computation.6 | async-start | bytes 147456 | tf_op jit(solution)/shard_map/reduce_scatter | solution.py:141
Sparse Core Ops, SparseCore 0:
  87.8 10.7 reduce-scatter.2
  100.9 9.9 reduce-scatter.4
where the time goes:
time: 120 us; the launch traced here: 119 us
  waiting for transfers between devices  42.5 us (35%)
  local copies, waits for them, and re-layouts  19.5 us (16%)
  matrix products  19.4 us (16%)
  starting transfers between devices  17.5 us (15%)
  between operations  13.6 us (11%)
  other arithmetic  6.36 us (5%)
    all_to_all x1, waiting for transfers between devices, body(): lax.all_to_all(send_tiles, 'sky', split_axis=0, concat_axis=0, tiled=True)  18.6 us
    reduce_scatter x1, waiting for transfers between devices, body(): lax.psum_scatter(weight_sum.astype(jnp.bfloat16), 'exp', scatter_dimensio...  12.2 us
    reduce_scatter x1, waiting for transfers between devices, body(): lax.psum_scatter(numerator.astype(jnp.bfloat16), 'exp', scatter_dimension...  9.76 us
    dot_general x6, matrix products, match_and_warp(): jnp.einsum('nij,nkj->nik', halfway, col_warp, preferred_element_type=jnp....  8.12 us
    all_to_all x1, starting transfers between devices, body(): lax.all_to_all(send_slots, 'sky', split_axis=0, concat_axis=0, tiled=True)  7.36 us
    dot_general x6, matrix products, match_and_warp(): jnp.einsum('nbij,bjk->nik', scaled, col_toeplitz, preferred_element_type=...  6.81 us
    all_to_all x1, starting transfers between devices, body(): lax.all_to_all(send_tiles, 'sky', split_axis=0, concat_axis=0, tiled=True)  5.98 us
    dynamic_slice x12, local copies, waits for them, and re-layouts, body(): lax.map(match_and_warp, grouped).reshape(tiles_dev, tile_rows * tile_cols)  5.64 us
  transfers between devices with their start and end apart: 5, of which 4 were waited for; matrix products, arithmetic and copies ran while one was open for 30% of the time, Pallas kernels for 0%

commit v1 on v0

v1 whole, which is shorter than its diff:
```python
import functools

import jax
import jax.numpy as jnp
from jax import lax
from jax.experimental import pallas as pl
from jax.experimental.pallas import tpu as pltpu
from jax.sharding import PartitionSpec as P

SLOTS = 16
META = 16
GROUP = 16
MESH = pl.DeviceIdType.MESH
VMEM_BYTES = 48 * 1024 * 1024


def toeplitz(basis_vals, distance):
    kernel_len = basis_vals.shape[1]
    picks = (distance[:, :, None] == jnp.arange(kernel_len, dtype=jnp.int32)[None, None, :]).astype(
        jnp.float32
    )
    return jnp.einsum("xyk,bk->bxy", picks, basis_vals.astype(jnp.float32))


def build_tables(basis_rows, basis_cols, tile_rows, tile_cols):
    kernel_len = basis_rows.shape[1]
    out_rows = jnp.arange(tile_rows, dtype=jnp.int32)
    in_rows = jnp.arange(tile_rows + kernel_len - 1, dtype=jnp.int32)
    out_cols = jnp.arange(tile_cols, dtype=jnp.int32)
    in_cols = jnp.arange(2 * tile_cols, dtype=jnp.int32)
    row_table = toeplitz(basis_rows, in_rows[None, :] - out_rows[:, None])
    col_table = toeplitz(basis_cols, in_cols[:, None] - out_cols[None, :])
    return row_table.reshape(-1, row_table.shape[2]), col_table.astype(jnp.bfloat16).reshape(
        -1, tile_cols
    )


def band(taps, shift, length):
    count = taps.shape[0]
    width = taps.shape[1]
    source = lax.broadcasted_iota(jnp.int32, (length, width), 0)
    position = lax.broadcasted_iota(jnp.int32, (length, width), 1)
    offset = source - jnp.clip(position + (shift - count // 2), 0, length - count)
    matrix = jnp.zeros((length, width), jnp.float32)
    for k in range(count):
        matrix = jnp.where(offset == k, taps[k : k + 1, :], matrix)
    return matrix.astype(jnp.bfloat16)


def tiles_kernel(
    capacity,
    tiles,
    coefs,
    row_taps,
    col_taps,
    shifts,
    words,
    weights,
    dest,
    slots,
    row_table,
    col_table,
    send,
    left,
    right,
    scaled,
    prod,
    meta,
    index,
    count,
):
    tile_count = tiles.shape[0]
    basis_count = coefs.shape[1]
    tile_rows = row_taps.shape[2]
    tile_cols = col_taps.shape[2]
    in_rows = row_table.shape[1]
    in_cols = tiles.shape[1] // in_rows
    owners = send.shape[0]
    blocks = tiles.shape[1] // 128

    def clear_index(p, carry):
        index[p] = tile_count
        return carry

    def clear_count(p, carry):
        count[p] = 0
        return carry

    lax.fori_loop(0, owners * capacity, clear_index, 0)
    lax.fori_loop(0, owners, clear_count, 0)

    def place(t, carry):
        owner = dest[t, 0]
        rank = count[owner]
        index[owner * capacity + rank] = t
        count[owner] = rank + 1
        return carry

    lax.fori_loop(0, tile_count, place, 0)
    lane = lax.broadcasted_iota(jnp.int32, (1, 128), 1)
    cell = (lax.broadcasted_iota(jnp.int32, (tile_rows, tile_cols), 0) // (tile_rows // 4)) * 8 + (
        lax.broadcasted_iota(jnp.int32, (tile_rows, tile_cols), 1) // (tile_cols // 8)
    )
    prod[tile_count] = jnp.zeros((tile_rows, tile_cols), jnp.float32)
    meta[tile_count] = jnp.where(lane == 32, 2.0 * SLOTS, jnp.zeros((1, 128), jnp.float32))

    def group(g, carry):
        first = pl.multiple_of(g * GROUP, GROUP)
        for r in range(in_rows):
            a, off = (in_cols * r) // 128, (in_cols * r) % 128
            z = min(a + 3, blocks)
            part = tiles[pl.ds(first, GROUP), a * 128 : z * 128].astype(jnp.float32)
            if off:
                part = pltpu.roll(part, (z - a) * 128 - off, 1)
            left[pl.ds(r, GROUP, stride=in_rows), :] = part[:, :128]
            right[pl.ds(r, GROUP, stride=in_rows), :] = part[:, 128:256]

        def pair(p, inner):
            passes = []
            for half in range(2):
                t = first + 2 * p + half
                base = pl.multiple_of((2 * p + half) * in_rows, in_rows)
                image = jnp.concatenate(
                    [left[pl.ds(base, in_rows), :], right[pl.ds(base, in_rows), :]], axis=1
                ).astype(jnp.bfloat16)
                factors = jnp.concatenate(
                    [
                        row_table[b * tile_rows : (b + 1) * tile_rows, :] * coefs[t, b]
                        for b in range(basis_count)
                    ],
                    axis=0,
                ).astype(jnp.bfloat16)
                passes.append(jnp.dot(factors, image, preferred_element_type=jnp.float32))
            rows = pl.ds(pl.multiple_of(p * 2 * tile_rows, 2 * tile_rows), 2 * tile_rows)
            for b in range(basis_count):
                both = jnp.concatenate(
                    [x[b * tile_rows : (b + 1) * tile_rows, :] for x in passes], axis=0
                )
                scaled[rows, b * 256 : (b + 1) * 256] = both.astype(jnp.bfloat16)
            return inner

        lax.fori_loop(0, GROUP // 2, pair, 0, unroll=2)
        matched = jnp.dot(scaled[...], col_table[...], preferred_element_type=jnp.float32)
        for u in range(GROUP):
            t = first + u
            own = matched[u * tile_rows : (u + 1) * tile_rows, :].astype(jnp.bfloat16)
            row_warp = band(row_taps[t].astype(jnp.float32), shifts[t, 0], tile_rows)
            col_warp = band(col_taps[t].astype(jnp.float32), shifts[t, 1], tile_cols)
            halfway = lax.dot_general(
                row_warp, own, (((0,), (0,)), ((), ())), preferred_element_type=jnp.float32
            ).astype(jnp.bfloat16)
            warped = jnp.dot(halfway, col_warp, preferred_element_type=jnp.float32)
            word, weight = words[t], weights[t]
            good = jnp.bitwise_and(jnp.right_shift(word, cell), 1) == 0
            prod[t] = jnp.where(good, warped * weight, 0.0)
            fine = jnp.bitwise_and(jnp.right_shift(word, jnp.minimum(lane, 31)), 1) == 0
            cells = jnp.where((lane < 32) & fine, weight, 0.0)
            meta[t] = jnp.where(lane == 32, slots[t].astype(jnp.float32), cells)
        return carry

    lax.fori_loop(0, tile_count // GROUP, group, 0)

    def dispatch(owner, carry):
        picks = [index[owner * capacity + r] for r in range(capacity)]
        for r in range(0, capacity, 2):
            both = jnp.concatenate([prod[picks[r]], prod[picks[r + 1]]], axis=0)
            send[owner, r * tile_rows : (r + 2) * tile_rows, :] = both.astype(jnp.bfloat16)
        rows = [meta[k] for k in picks]
        rows.append(jnp.zeros((META - capacity, 128), jnp.float32))
        send[owner, capacity * tile_rows :, :] = jnp.concatenate(rows, axis=0).astype(jnp.bfloat16)
        return carry

    lax.fori_loop(0, owners, dispatch, 0)


def stack_kernel(
    sky, exp, capacity, tile_rows, send, out, held, part, part_held, own_sem, sky_send, sky_recv,
    exp_send, exp_recv
):
    me = lax.axis_index("sky")
    mine = lax.axis_index("exp")
    chunk = send.shape[1]
    share = SLOTS // exp
    body_rows = share * tile_rows
    barrier = pltpu.get_barrier_semaphore()
    for k in range(1, sky):
        pl.semaphore_signal(
            barrier, inc=1, device_id=(lax.rem(me + k, sky), mine), device_id_type=MESH
        )
    for k in range(1, exp):
        pl.semaphore_signal(
            barrier, inc=1, device_id=(me, lax.rem(mine + k, exp)), device_id_type=MESH
        )
    pl.semaphore_wait(barrier, sky + exp - 2)
    copies = []
    order = sorted(range(1, sky), key=lambda k: -min(k, sky - k))
    for k in order:
        owner = lax.rem(me + k, sky)
        copy = pltpu.make_async_remote_copy(
            src_ref=send.at[owner],
            dst_ref=held.at[k],
            send_sem=sky_send.at[k],
            recv_sem=sky_recv.at[k],
            device_id=(owner, mine),
            device_id_type=MESH,
        )
        copy.start()
        copies.append(copy)
    local = pltpu.make_async_copy(send.at[me], held.at[0], own_sem)
    local.start()
    total = sky * chunk
    place = lax.broadcasted_iota(jnp.int32, (1, total), 1)
    source = place // chunk
    within = place - source * chunk
    used = within < capacity * tile_rows
    rank = within // tile_rows
    pixel_row = (within - rank * tile_rows).astype(jnp.float32)
    label = jnp.where(used, source * 8 + rank, -1)
    spread = jnp.where(
        lax.broadcasted_iota(jnp.int32, (sky * 8, total), 0) == label, 1.0, 0.0
    ).astype(jnp.bfloat16)
    local.wait()
    for copy in copies:
        copy.wait()
    info = jnp.concatenate(
        [held[k, capacity * tile_rows :, :].astype(jnp.float32)[:8] for k in range(sky)], axis=0
    )
    which = lax.broadcasted_iota(jnp.int32, (8, sky * 8), 1) % 8
    slot_row = jnp.where(which < capacity, info.T[32:40, :], 2.0 * SLOTS)
    lane_slot = jnp.dot(
        slot_row.astype(jnp.bfloat16), spread, preferred_element_type=jnp.float32
    )[0:1, :]
    goal = jnp.where(used, lane_slot * tile_rows + pixel_row, -1.0)
    out_row = lax.broadcasted_iota(jnp.int32, (SLOTS * tile_rows, total), 0).astype(jnp.float32)
    pick = jnp.where(out_row == goal, 1.0, 0.0).astype(jnp.bfloat16)
    numerator = jnp.dot(
        pick, held[...].reshape(total, held.shape[2]), preferred_element_type=jnp.float32
    )
    slot_pick = jnp.where(
        lax.broadcasted_iota(jnp.int32, (SLOTS, sky * 8), 0).astype(jnp.float32)
        == slot_row[0:1, :],
        1.0,
        0.0,
    ).astype(jnp.bfloat16)
    sums = jnp.dot(slot_pick, info.astype(jnp.bfloat16), preferred_element_type=jnp.float32)
    pad = jnp.zeros((META - share, 128), jnp.float32)
    for e in range(exp):
        part[e, :body_rows, :] = numerator[e * body_rows : (e + 1) * body_rows, :].astype(
            jnp.bfloat16
        )
        part[e, body_rows:, :] = jnp.concatenate(
            [sums[e * share : (e + 1) * share, :], pad], axis=0
        ).astype(jnp.bfloat16)
    swaps = []
    for k in range(1, exp):
        other = lax.rem(mine + k, exp)
        swap = pltpu.make_async_remote_copy(
            src_ref=part.at[other],
            dst_ref=part_held.at[k - 1],
            send_sem=exp_send.at[k - 1],
            recv_sem=exp_recv.at[k - 1],
            device_id=(me, other),
            device_id_type=MESH,
        )
        swap.start()
        swaps.append(swap)
    whole = part[mine].astype(jnp.float32)
    for k, swap in enumerate(swaps):
        swap.wait()
        whole = whole + part_held[k].astype(jnp.float32)
    weight = whole[body_rows : body_rows + share, :]
    columns = out.shape[1]
    cell = lax.broadcasted_iota(jnp.int32, (128, 4 * columns), 0)
    target = lax.broadcasted_iota(jnp.int32, (128, 4 * columns), 1) // (columns // 8)
    widen = jnp.where(cell == target, 1.0, 0.0).astype(jnp.bfloat16)
    high = weight.astype(jnp.bfloat16)
    low = (weight - high.astype(jnp.float32)).astype(jnp.bfloat16)
    wide = jnp.dot(high, widen, preferred_element_type=jnp.float32) + jnp.dot(
        low, widen, preferred_element_type=jnp.float32
    )
    quarter = lax.broadcasted_iota(jnp.int32, (tile_rows, columns), 0) // (tile_rows // 4)
    for q in range(share):
        plane = jnp.zeros((tile_rows, columns), jnp.float32)
        for g in range(4):
            plane = jnp.where(quarter == g, wide[q : q + 1, g * columns : (g + 1) * columns], plane)
        rows = slice(q * tile_rows, (q + 1) * tile_rows)
        out[rows, :] = whole[rows, :] / jnp.maximum(plane, 1.0)


def body(
    padded_tiles,
    coefficients,
    row_taps,
    col_taps,
    shifts,
    mask_words,
    weights,
    destination,
    patch_slot,
    basis_rows,
    basis_cols,
):
    sky = lax.axis_size("sky")
    exp = lax.axis_size("exp")
    tile_count = padded_tiles.shape[0]
    tile_rows = row_taps.shape[2]
    tile_cols = col_taps.shape[2]
    basis_count, kernel_len = basis_rows.shape
    in_rows = tile_rows + kernel_len - 1
    capacity = 2 * ((tile_count + sky - 1) // sky)
    chunk = capacity * tile_rows + META
    row_table, col_table = build_tables(basis_rows, basis_cols, tile_rows, tile_cols)
    vmem = pl.BlockSpec(memory_space=pltpu.VMEM)
    smem = pl.BlockSpec(memory_space=pltpu.SMEM)
    send = pl.pallas_call(
        functools.partial(tiles_kernel, capacity),
        out_shape=jax.ShapeDtypeStruct((sky, chunk, tile_cols), jnp.bfloat16),
        in_specs=[vmem, smem, vmem, vmem, smem, smem, smem, smem, smem, vmem, vmem],
        out_specs=vmem,
        scratch_shapes=[
            pltpu.VMEM((GROUP * in_rows, 128), jnp.float32),
            pltpu.VMEM((GROUP * in_rows, 128), jnp.float32),
            pltpu.VMEM((GROUP * tile_rows, basis_count * 256), jnp.bfloat16),
            pltpu.VMEM((tile_count + 1, tile_rows, tile_cols), jnp.float32),
            pltpu.VMEM((tile_count + 1, 1, 128), jnp.float32),
            pltpu.SMEM((sky * capacity,), jnp.int32),
            pltpu.SMEM((sky,), jnp.int32),
        ],
        compiler_params=pltpu.CompilerParams(vmem_limit_bytes=VMEM_BYTES),
        name="tiles",
    )(
        padded_tiles,
        coefficients,
        row_taps,
        col_taps,
        shifts,
        mask_words,
        weights.astype(jnp.float32),
        destination,
        patch_slot,
        row_table,
        col_table,
    )
    share_rows = SLOTS // exp * tile_rows
    return pl.pallas_call(
        functools.partial(stack_kernel, sky, exp, capacity, tile_rows),
        out_shape=jax.ShapeDtypeStruct((share_rows, tile_cols), jnp.float32),
        in_specs=[vmem],
        out_specs=vmem,
        scratch_shapes=[
            pltpu.VMEM((sky, chunk, tile_cols), jnp.bfloat16),
            pltpu.VMEM((exp, share_rows + META, tile_cols), jnp.bfloat16),
            pltpu.VMEM((max(exp - 1, 1), share_rows + META, tile_cols), jnp.bfloat16),
            pltpu.SemaphoreType.DMA,
            pltpu.SemaphoreType.DMA((sky,)),
            pltpu.SemaphoreType.DMA((sky,)),
            pltpu.SemaphoreType.DMA((max(exp - 1, 1),)),
            pltpu.SemaphoreType.DMA((max(exp - 1, 1),)),
        ],
        compiler_params=pltpu.CompilerParams(
            collective_id=0, has_side_effects=True, vmem_limit_bytes=VMEM_BYTES
        ),
        name="stack",
    )(send)


def solution(mesh):
    placed = (
        P(("sky", "exp"), None),
        P(("sky", "exp"), None),
        P(("sky", "exp"), None, None),
        P(("sky", "exp"), None, None),
        P(("sky", "exp"), None),
        P(("sky", "exp")),
        P(("sky", "exp")),
        P(("sky", "exp"), None),
        P(("sky", "exp")),
        P(),
        P(),
    )
    return jax.shard_map(
        body, mesh=mesh, in_specs=placed, out_specs=P(("sky", "exp"), None), check_vma=False
    )
```

time: 120 us -> 50.5 us (0.42)
  Pallas kernels: 0 us -> 46 us
  waiting for transfers between devices: 42.5 us -> 0 us
  matrix products: 19.4 us -> 1.67 us
  starting transfers between devices: 17.5 us -> 0 us
  local copies, waits for them, and re-layouts: 19.5 us -> 2.4 us
  between operations: 13.6 us -> 0.18 us
  other arithmetic: 6.36 us -> 0.02 us
    pallas_call x0 -> x2, Pallas kernels: none -> 46 us  [the longest x1 24.9 us: body(): pl.pallas_call(functools.partial(stack_kernel, sky, exp, capacity, tile_r...]
    reduce_scatter x2 -> x0, waiting for transfers between devices: 22 us -> none  [the longest x1 12.2 us: body(): lax.psum_scatter(weight_sum.astype(jnp.bfloat16), 'exp', scatter_dimensio...]
    all_to_all x3 -> x0, waiting for transfers between devices: 20.5 us -> none  [the longest x1 18.6 us: body(): lax.all_to_all(send_tiles, 'sky', split_axis=0, concat_axis=0, tiled=True)]
    dot_general x19 -> x2, matrix products: 19.4 us -> 1.67 us  [toeplitz(): return jnp.einsum('xyk,bk->bxy', picks, basis_vals.astype(jnp.float32))]
    all_to_all x3 -> x0, starting transfers between devices: 17.4 us -> none  [the longest x1 7.36 us: body(): lax.all_to_all(send_slots, 'sky', split_axis=0, concat_axis=0, tiled=True)]
    dynamic_slice x12 -> x0, local copies, waits for them, and re-layouts: 5.64 us -> none  [body(): lax.map(match_and_warp, grouped).reshape(tiles_dev, tile_rows * tile_cols)]
    reshape x7 -> x0, local copies, waits for them, and re-layouts: 4.56 us -> none  [the longest x6 4.48 us: match_and_warp(): padded.reshape(per_block, tile_rows + kernel_len - 1, tile_cols + kernel_...]
    squeeze x12 -> x0, local copies, waits for them, and re-layouts: 4.31 us -> none  [body(): lax.map(match_and_warp, grouped).reshape(tiles_dev, tile_rows * tile_cols)]
  transfers between devices with their start and end apart: 5 -> 0, of which waited for: 4 -> 0; matrix products, arithmetic and copies ran while one was open for 30% -> 0% of each run, Pallas kernels for 0% -> 0%
where the time goes in v1:
time: 50.5 us; the launch traced here: 50.3 us
  Pallas kernels  46 us (91%)
  local copies, waits for them, and re-layouts  2.4 us (5%)
  matrix products  1.67 us (3%)
    pallas_call x1, Pallas kernels, body(): pl.pallas_call(functools.partial(stack_kernel, sky, exp, capacity, tile_r...  24.9 us
    pallas_call x1, Pallas kernels, body(): pl.pallas_call(functools.partial(tiles_kernel, capacity), out_shape=jax.S...  21.2 us
    unnamed x28, local copies, waits for them, and re-layouts  2.09 us
    dot_general x2, matrix products, toeplitz(): return jnp.einsum('xyk,bk->bxy', picks, basis_vals.astype(jnp.float32))  1.67 us

profile of v1, /device:TPU:0, one launch (start us, length us, event | category | flops | bytes accessed | tf_op | source)
XLA Modules:
  0.0 50.3 jit_solution(3318086210338120360)
XLA Ops:
  0.0 0.0 copy-start
  0.0 0.7 %copy-done = bf16[20,41]{1,0:T(8,128)(2,1)S(1)} copy-done((bf16[20,41]{1,0:T(8,128)(2,1)S(1)}, bf16[20,41]{1,0:T(8,128)(2,1)}, u32[]{:S(2)}) %copy-start) | copy-done | bytes 1664
  0.7 1.5 %fusion.3 = bf16[20,256,128]{2,0,1:T(8,128)(2,1)S(1)} fusion(s32[256,128]{1,0:T(8,128)S(1)} %iota_subtract_fusion, bf16[20,41]{1,0:T(8,128)(2,1)S(1)} %copy-done), kind=kOutput, calls=%fused_computation.4 | convolution fusion | flops 55738368 | bytes 1443432 | tf_op jit(solution)/shard_map/xyk,bk->bxy/dot_general | solution.py:22
  2.1 0.0 copy-start.5
  2.2 0.0 copy-start.4
  2.2 0.0 copy-start.6
  2.2 0.0 copy-start.8
  2.2 0.0 copy-start.9
  2.2 0.0 copy-start.10
  2.2 0.0 copy-start.1
  2.2 0.0 copy-start.2
  2.2 0.0 copy-start.3
  2.3 0.3 copy.13
  2.5 0.3 copy-done.7
  2.8 0.2 convolution_bitcast_fusion
  3.1 0.0 copy-done.5
  3.1 0.1 copy.15.row_taps
  3.2 0.0 copy-done.4
  3.3 0.1 copy.14.coefs
  3.4 0.1 copy.17.shifts
  3.5 0.1 copy.18.dest
  3.6 21.2 %tiles.2.send = bf16[16,160,128]{2,1,0:T(8,128)(2,1)S(1)} custom-call(bf16[48,10752]{1,0:T(8,128)(2,1)S(1)} %copy-done.1, f32[48,20]{1,0:T(8,128)S(1)} %copy.14.coefs, bf16[48,6,24]{2,1,0:T(8,128)(2,1)S(1)} %copy.15.row_taps, bf16[48,6,128]{2,1,0:T(8,128)(2,1)S(1)} %copy.16.col_taps, s32[48,2]{1,0:T(8,128)S(1)} %copy.17.shifts, s32[48]{0:T(128)S(1)} %copy-done.2, ...), custom_call_target="tpu_custom_call" | custom-call | tf_op jit(solution)/shard_map/tiles/pallas_call | solution.py:315
  24.8 24.9 %stack.1 = f32[192,128]{1,0:T(8,128)S(1)} custom-call(bf16[16,160,128]{2,1,0:T(8,128)(2,1)S(1)} %tiles.2.send), custom_call_target="tpu_custom_call" | custom-call | tf_op jit(solution)/shard_map/stack/pallas_call | solution.py:345
  49.6 0.6 %copy.20 = f32[192,128]{1,0:T(8,128)} copy(f32[192,128]{1,0:T(8,128)S(1)} %stack.1) | data formatting | bytes 196608
  (13 shorter events, 0.1 us)
Async XLA Ops:
  0.0 0.7 %copy-start = (bf16[20,41]{1,0:T(8,128)(2,1)S(1)}, bf16[20,41]{1,0:T(8,128)(2,1)}, u32[]{:S(2)}) copy-start(bf16[20,41]{1,0:T(8,128)(2,1)} %param.21) | copy-start | bytes 4924
  2.1 0.7 %copy-start.7 = (bf16[20,41]{1,0:T(8,128)(2,1)S(1)}, bf16[20,41]{1,0:T(8,128)(2,1)}, u32[]{:S(2)}) copy-start(bf16[20,41]{1,0:T(8,128)(2,1)} %param.20) | copy-start | bytes 4924
  2.1 1.0 %copy-start.5 = (bf16[48,6,24]{0,2,1:T(8,128)(2,1)S(1)}, bf16[48,6,24]{0,2,1:T(8,128)(2,1)}, u32[]{:S(2)}) copy-start(bf16[48,6,24]{0,2,1:T(8,128)(2,1)} %param.13) | copy-start | bytes 41476
  2.2 1.1 %copy-start.4 = (bf16[48,6,128]{2,0,1:T(8,128)(2,1)S(1)}, bf16[48,6,128]{2,0,1:T(8,128)(2,1)}, u32[]{:S(2)}) copy-start(bf16[48,6,128]{2,0,1:T(8,128)(2,1)} %param.14) | copy-start | bytes 221188
  2.2 1.1 %copy-start.6 = (f32[48,20]{0,1:T(8,128)S(1)}, f32[48,20]{0,1:T(8,128)}, u32[]{:S(2)}) copy-start(f32[48,20]{0,1:T(8,128)} %param.12) | copy-start | bytes 11524
  2.2 1.2 %copy-start.8 = (s32[48,2]{0,1:T(2,128)S(1)}, s32[48,2]{0,1:T(2,128)}, u32[]{:S(2)}) copy-start(s32[48,2]{0,1:T(2,128)} %param.15) | copy-start | bytes 1156
  2.2 1.3 %copy-start.9 = (s32[48,1]{0,1:T(1,128)S(1)}, s32[48,1]{0,1:T(1,128)}, u32[]{:S(2)}) copy-start(s32[48,1]{0,1:T(1,128)} %param.18) | copy-start | bytes 580
  2.2 1.4 %copy-start.10 = (bf16[48]{0:T(256)(128)(2,1)S(1)}, bf16[48]{0:T(256)(128)(2,1)}, u32[]{:S(2)}) copy-start(bf16[48]{0:T(256)(128)(2,1)} %param.17) | copy-start | bytes 292
  2.2 1.4 %copy-start.1 = (bf16[48,10752]{1,0:T(8,128)(2,1)S(1)}, bf16[48,10752]{1,0:T(8,128)(2,1)}, u32[]{:S(2)}) copy-start(bf16[48,10752]{1,0:T(8,128)(2,1)} %tiles.3) | copy-start | bytes 3096580
  2.2 1.4 %copy-start.2 = (s32[48]{0:T(128)S(1)}, s32[48]{0:T(128)}, u32[]{:S(2)}) copy-start(s32[48]{0:T(128)} %words.1) | copy-start | bytes 580
  2.2 1.4 %copy-start.3 = (s32[48]{0:T(128)S(1)}, s32[48]{0:T(128)}, u32[]{:S(2)}) copy-start(s32[48]{0:T(128)} %slots.1) | copy-start | bytes 580

commit v2 on v1

v2 whole, which is shorter than its diff:
```python
import functools

import jax
import jax.numpy as jnp
from jax import lax
from jax.experimental import pallas as pl
from jax.experimental.pallas import tpu as pltpu
from jax.sharding import PartitionSpec as P

SLOTS = 16
META = 16
GROUP = 16
MESH = pl.DeviceIdType.MESH
VMEM_BYTES = 48 * 1024 * 1024


def plan_kernel(
    sky, capacity, me, dest, rows, cols, plan, row_table, col_table
):
    count = dest.shape[1]
    basis_count = rows.shape[0]
    tile_rows = row_table.shape[0] // basis_count
    tile_cols = col_table.shape[1]
    lane = lax.broadcasted_iota(jnp.int32, (128, 128), 1)
    line = lax.broadcasted_iota(jnp.int32, (128, 128), 0)
    visit = sky - 1 - jnp.bitwise_xor(dest[...], me[0])
    visit = jnp.concatenate([visit, jnp.full((1, 128 - count), sky, jnp.int32)], axis=1)
    visit_across = jnp.broadcast_to(visit, (128, 128))
    visit_down = visit_across.astype(jnp.float32).T.astype(jnp.int32)
    ahead = (visit_down < visit_across) | ((visit_down == visit_across) & (line < lane))
    position = jnp.sum(ahead.astype(jnp.float32), axis=0, keepdims=True)
    position_down = jnp.broadcast_to(position, (128, 128)).T.astype(jnp.int32)
    order = jnp.sum(jnp.where(position_down == lane, line, 0).astype(jnp.float32), axis=0, keepdims=True)
    chunk, rank = lane // capacity, lane % capacity
    start = jnp.sum((visit_down < chunk).astype(jnp.float32), axis=0, keepdims=True)
    held = jnp.sum((visit_down == chunk).astype(jnp.float32), axis=0, keepdims=True)
    rank = rank[0:1, :].astype(jnp.float32)
    place = jnp.where(rank < held, start + rank, float(count))
    plan[...] = jnp.concatenate(
        [order, place, jnp.zeros((6, 128), jnp.float32)], axis=0
    ).astype(jnp.int32)
    for b in range(basis_count):
        row = jnp.broadcast_to(rows[b : b + 1, :], (tile_rows, 128))
        row_table[b * tile_rows : (b + 1) * tile_rows, :] = pltpu.roll(
            row, 0, 1, stride=1, stride_axis=0
        )
        col = jnp.broadcast_to(cols[b : b + 1, :], (128, 128))
        col = pltpu.roll(col, 0, 1, stride=1, stride_axis=0)
        col_table[b * 256 : b * 256 + 128, :] = jnp.where(line >= lane, col, 0.0).astype(jnp.bfloat16)
        col_table[b * 256 + 128 : (b + 1) * 256, :] = jnp.where(line < lane, col, 0.0).astype(
            jnp.bfloat16
        )


def band(taps, shift, length):
    count = taps.shape[0]
    width = taps.shape[1]
    source = lax.broadcasted_iota(jnp.int32, (length, width), 0)
    position = lax.broadcasted_iota(jnp.int32, (length, width), 1)
    offset = source - jnp.clip(position + (shift - count // 2), 0, length - count)
    matrix = jnp.zeros((length, width), jnp.float32)
    for k in range(count):
        matrix = jnp.where(offset == k, taps[k : k + 1, :], matrix)
    return matrix.astype(jnp.bfloat16)


def peer(me, m):
    bit, other = 1, me
    while bit <= m:
        if m & bit:
            other = other + bit * (1 - 2 * lax.rem(me // bit, 2))
        bit *= 2
    return other


def stack_kernel(
    sky,
    exp,
    capacity,
    tiles,
    coefs,
    row_taps,
    col_taps,
    shifts,
    words,
    weights,
    slots,
    plan,
    row_table,
    col_table,
    out,
    left,
    right,
    images,
    scaled,
    prod,
    meta,
    send,
    held,
    part,
    part_held,
    sky_send,
    sky_recv,
    exp_send,
    exp_recv,
):
    me = lax.axis_index("sky")
    mine = lax.axis_index("exp")
    barrier = pltpu.get_barrier_semaphore()
    for m in range(1, sky):
        pl.semaphore_signal(barrier, inc=1, device_id=(peer(me, m), mine), device_id_type=MESH)
    for k in range(1, exp):
        pl.semaphore_signal(
            barrier, inc=1, device_id=(me, lax.rem(mine + k, exp)), device_id_type=MESH
        )
    tile_count = tiles.shape[0]
    basis_count = coefs.shape[0]
    tile_rows = row_taps.shape[2]
    tile_cols = col_taps.shape[2]
    in_rows = images.shape[1]
    in_cols = tiles.shape[1] // in_rows
    blocks = tiles.shape[1] // 128
    chunk = held.shape[1]
    share = SLOTS // exp
    body_rows = share * tile_rows
    lane = lax.broadcasted_iota(jnp.int32, (1, 128), 1)
    cell = (lax.broadcasted_iota(jnp.int32, (tile_rows, tile_cols), 0) // (tile_rows // 4)) * 8 + (
        lax.broadcasted_iota(jnp.int32, (tile_rows, tile_cols), 1) // (tile_cols // 8)
    )
    prod[tile_count] = jnp.zeros((tile_rows, tile_cols), jnp.float32)
    meta[tile_count] = jnp.where(lane == 32, 2.0 * SLOTS, jnp.zeros((1, 128), jnp.float32))

    def unfold(g, carry):
        first = pl.multiple_of(g * GROUP, GROUP)
        for r in range(in_rows):
            a, off = (in_cols * r) // 128, (in_cols * r) % 128
            z = min(a + 3, blocks)
            part_row = tiles[pl.ds(first, GROUP), a * 128 : z * 128].astype(jnp.float32)
            if off:
                part_row = pltpu.roll(part_row, (z - a) * 128 - off, 1)
            left[pl.ds(r, GROUP, stride=in_rows), :] = part_row[:, :128]
            right[pl.ds(r, GROUP, stride=in_rows), :] = part_row[:, 128:256]
        for u in range(GROUP):
            rows = slice(u * in_rows, (u + 1) * in_rows)
            images[first + u] = jnp.concatenate([left[rows, :], right[rows, :]], axis=1).astype(
                jnp.bfloat16
            )
        return carry

    lax.fori_loop(0, tile_count // GROUP, unfold, 0)
    copies, done = [], 0
    for g in range(tile_count // GROUP):
        first = g * GROUP

        def pair(p, inner, first=first):
            passes = []
            for half in range(2):
                t = plan[0, first + 2 * p + half]
                factors = jnp.concatenate(
                    [
                        row_table[b * tile_rows : (b + 1) * tile_rows, :in_rows] * coefs[b, t]
                        for b in range(basis_count)
                    ],
                    axis=0,
                ).astype(jnp.bfloat16)
                passes.append(jnp.dot(factors, images[t], preferred_element_type=jnp.float32))
            rows = pl.ds(pl.multiple_of(p * 2 * tile_rows, 2 * tile_rows), 2 * tile_rows)
            for b in range(basis_count):
                both = jnp.concatenate(
                    [x[b * tile_rows : (b + 1) * tile_rows, :] for x in passes], axis=0
                )
                scaled[rows, b * 256 : (b + 1) * 256] = both.astype(jnp.bfloat16)
            return inner

        lax.fori_loop(0, GROUP // 2, pair, 0, unroll=2)
        matched = jnp.dot(scaled[...], col_table[...], preferred_element_type=jnp.float32)
        for u in range(GROUP):
            t = plan[0, first + u]
            own = matched[u * tile_rows : (u + 1) * tile_rows, :].astype(jnp.bfloat16)
            row_warp = band(row_taps[t].astype(jnp.float32), shifts[0, t], tile_rows)
            col_warp = band(col_taps[t].astype(jnp.float32), shifts[1, t], tile_cols)
            halfway = lax.dot_general(
                row_warp, own, (((0,), (0,)), ((), ())), preferred_element_type=jnp.float32
            ).astype(jnp.bfloat16)
            warped = jnp.dot(halfway, col_warp, preferred_element_type=jnp.float32)
            word, weight = words[t], weights[t]
            good = jnp.bitwise_and(jnp.right_shift(word, cell), 1) == 0
            prod[first + u] = jnp.where(good, warped * weight, 0.0)
            fine = jnp.bitwise_and(jnp.right_shift(word, jnp.minimum(lane, 31)), 1) == 0
            cells = jnp.where((lane < 32) & fine, weight, 0.0)
            meta[first + u] = jnp.where(lane == 32, slots[t].astype(jnp.float32), cells)
        if g == 0:
            pl.semaphore_wait(barrier, sky + exp - 2)
        finished = first + GROUP
        ready = sky if finished == tile_count else min(sky, finished // capacity)
        for v in range(done, ready):
            target = held if v == sky - 1 else send
            picks = [plan[1, v * capacity + r] for r in range(capacity)]
            for r in range(0, capacity, 2):
                both = jnp.concatenate([prod[picks[r]], prod[picks[r + 1]]], axis=0)
                target[v, r * tile_rows : (r + 2) * tile_rows, :] = both.astype(jnp.bfloat16)
            rows = [meta[k] for k in picks]
            rows.append(jnp.zeros((META - capacity, 128), jnp.float32))
            target[v, capacity * tile_rows :, :] = jnp.concatenate(rows, axis=0).astype(
                jnp.bfloat16
            )
            if v < sky - 1:
                copy = pltpu.make_async_remote_copy(
                    src_ref=send.at[v],
                    dst_ref=held.at[v],
                    send_sem=sky_send.at[v],
                    recv_sem=sky_recv.at[v],
                    device_id=(peer(me, sky - 1 - v), mine),
                    device_id_type=MESH,
                )
                copy.start()
                copies.append(copy)
        done = ready
    half = sky // 2
    total = half * chunk
    place = lax.broadcasted_iota(jnp.int32, (1, total), 1)
    source = place // chunk
    within = place - source * chunk
    used = within < capacity * tile_rows
    rank = within // tile_rows
    pixel_row = (within - rank * tile_rows).astype(jnp.float32)
    label = jnp.where(used, source * 8 + rank, -1)
    spread = jnp.where(
        lax.broadcasted_iota(jnp.int32, (half * 8, total), 0) == label, 1.0, 0.0
    ).astype(jnp.bfloat16)
    out_row = lax.broadcasted_iota(jnp.int32, (SLOTS * tile_rows, total), 0).astype(jnp.float32)
    slot_of = lax.broadcasted_iota(jnp.int32, (SLOTS, half * 8), 0).astype(jnp.float32)
    which = lax.broadcasted_iota(jnp.int32, (8, half * 8), 1) % 8
    numerator = sums = None
    for h in range(2):
        for copy in copies[h * half : (h + 1) * half]:
            copy.wait()
        span = range(h * half, (h + 1) * half)
        info = jnp.concatenate(
            [held[k, capacity * tile_rows :, :].astype(jnp.float32)[:8] for k in span], axis=0
        )
        slot_row = jnp.where(which < capacity, info.T[32:40, :], 2.0 * SLOTS)
        lane_slot = jnp.dot(
            slot_row.astype(jnp.bfloat16), spread, preferred_element_type=jnp.float32
        )[0:1, :]
        goal = jnp.where(used, lane_slot * tile_rows + pixel_row, -1.0)
        pick = jnp.where(out_row == goal, 1.0, 0.0).astype(jnp.bfloat16)
        block = held[h * half : (h + 1) * half].reshape(total, held.shape[2])
        more = jnp.dot(pick, block, preferred_element_type=jnp.float32)
        slot_pick = jnp.where(slot_of == slot_row[0:1, :], 1.0, 0.0).astype(jnp.bfloat16)
        extra = jnp.dot(slot_pick, info.astype(jnp.bfloat16), preferred_element_type=jnp.float32)
        numerator = more if h == 0 else numerator + more
        sums = extra if h == 0 else sums + extra
    pad = jnp.zeros((META - share, 128), jnp.float32)
    for e in range(exp):
        part[e, :body_rows, :] = numerator[e * body_rows : (e + 1) * body_rows, :].astype(
            jnp.bfloat16
        )
        part[e, body_rows:, :] = jnp.concatenate(
            [sums[e * share : (e + 1) * share, :], pad], axis=0
        ).astype(jnp.bfloat16)
    swaps = []
    for k in range(1, exp):
        other = lax.rem(mine + k, exp)
        swap = pltpu.make_async_remote_copy(
            src_ref=part.at[other],
            dst_ref=part_held.at[k - 1],
            send_sem=exp_send.at[k - 1],
            recv_sem=exp_recv.at[k - 1],
            device_id=(me, other),
            device_id_type=MESH,
        )
        swap.start()
        swaps.append(swap)
    whole = part[mine].astype(jnp.float32)
    for k, swap in enumerate(swaps):
        swap.wait()
        whole = whole + part_held[k].astype(jnp.float32)
    weight = whole[body_rows : body_rows + share, :]
    columns = out.shape[1]
    cell = lax.broadcasted_iota(jnp.int32, (128, 4 * columns), 0)
    target = lax.broadcasted_iota(jnp.int32, (128, 4 * columns), 1) // (columns // 8)
    widen = jnp.where(cell == target, 1.0, 0.0).astype(jnp.bfloat16)
    high = weight.astype(jnp.bfloat16)
    low = (weight - high.astype(jnp.float32)).astype(jnp.bfloat16)
    wide = jnp.dot(high, widen, preferred_element_type=jnp.float32) + jnp.dot(
        low, widen, preferred_element_type=jnp.float32
    )
    quarter = lax.broadcasted_iota(jnp.int32, (tile_rows, columns), 0) // (tile_rows // 4)
    for q in range(share):
        plane = jnp.zeros((tile_rows, columns), jnp.float32)
        for g in range(4):
            plane = jnp.where(quarter == g, wide[q : q + 1, g * columns : (g + 1) * columns], plane)
        rows = slice(q * tile_rows, (q + 1) * tile_rows)
        out[rows, :] = whole[rows, :] / jnp.maximum(plane, 1.0)


def body(
    padded_tiles,
    coefficients,
    row_taps,
    col_taps,
    shifts,
    mask_words,
    weights,
    destination,
    patch_slot,
    basis_rows,
    basis_cols,
):
    sky = lax.axis_size("sky")
    exp = lax.axis_size("exp")
    tile_count = padded_tiles.shape[0]
    tile_rows = row_taps.shape[2]
    tile_cols = col_taps.shape[2]
    basis_count, kernel_len = basis_rows.shape
    in_rows = tile_rows + kernel_len - 1
    capacity = 2 * ((tile_count + sky - 1) // sky)
    chunk = capacity * tile_rows + META
    vmem = pl.BlockSpec(memory_space=pltpu.VMEM)
    smem = pl.BlockSpec(memory_space=pltpu.SMEM)
    rows = jnp.pad(basis_rows, ((0, 0), (0, 128 - kernel_len))).astype(jnp.float32)
    cols = jnp.concatenate(
        [
            basis_cols[:, :1],
            jnp.zeros((basis_count, 128 - kernel_len), basis_cols.dtype),
            basis_cols[:, :0:-1],
        ],
        axis=1,
    ).astype(jnp.float32)
    plan, row_table, col_table = pl.pallas_call(
        functools.partial(plan_kernel, sky, capacity),
        out_shape=(
            jax.ShapeDtypeStruct((8, 128), jnp.int32),
            jax.ShapeDtypeStruct((basis_count * tile_rows, 128), jnp.float32),
            jax.ShapeDtypeStruct((basis_count * 256, tile_cols), jnp.bfloat16),
        ),
        in_specs=[smem, vmem, vmem, vmem],
        out_specs=(vmem, vmem, vmem),
        compiler_params=pltpu.CompilerParams(vmem_limit_bytes=VMEM_BYTES),
        name="plan",
    )(lax.axis_index("sky").reshape(1), destination.reshape(1, tile_count), rows, cols)
    share_rows = SLOTS // exp * tile_rows
    return pl.pallas_call(
        functools.partial(stack_kernel, sky, exp, capacity),
        out_shape=jax.ShapeDtypeStruct((share_rows, tile_cols), jnp.float32),
        in_specs=[vmem, smem, vmem, vmem, smem, smem, smem, smem, smem, vmem, vmem],
        out_specs=vmem,
        scratch_shapes=[
            pltpu.VMEM((GROUP * in_rows, 128), jnp.float32),
            pltpu.VMEM((GROUP * in_rows, 128), jnp.float32),
            pltpu.VMEM((tile_count, in_rows, 256), jnp.bfloat16),
            pltpu.VMEM((GROUP * tile_rows, basis_count * 256), jnp.bfloat16),
            pltpu.VMEM((tile_count + 1, tile_rows, tile_cols), jnp.float32),
            pltpu.VMEM((tile_count + 1, 1, 128), jnp.float32),
            pltpu.VMEM((sky - 1, chunk, tile_cols), jnp.bfloat16),
            pltpu.VMEM((sky, chunk, tile_cols), jnp.bfloat16),
            pltpu.VMEM((exp, share_rows + META, tile_cols), jnp.bfloat16),
            pltpu.VMEM((max(exp - 1, 1), share_rows + META, tile_cols), jnp.bfloat16),
            pltpu.SemaphoreType.DMA((sky - 1,)),
            pltpu.SemaphoreType.DMA((sky - 1,)),
            pltpu.SemaphoreType.DMA((max(exp - 1, 1),)),
            pltpu.SemaphoreType.DMA((max(exp - 1, 1),)),
        ],
        compiler_params=pltpu.CompilerParams(
            collective_id=0, has_side_effects=True, vmem_limit_bytes=VMEM_BYTES
        ),
        name="stack",
    )(
        padded_tiles,
        coefficients.T,
        row_taps,
        col_taps,
        shifts.T,
        mask_words,
        weights.astype(jnp.float32),
        patch_slot,
        plan,
        row_table,
        col_table,
    )


def solution(mesh):
    placed = (
        P(("sky", "exp"), None),
        P(("sky", "exp"), None),
        P(("sky", "exp"), None, None),
        P(("sky", "exp"), None, None),
        P(("sky", "exp"), None),
        P(("sky", "exp")),
        P(("sky", "exp")),
        P(("sky", "exp"), None),
        P(("sky", "exp")),
        P(),
        P(),
    )
    return jax.shard_map(
        body, mesh=mesh, in_specs=placed, out_specs=P(("sky", "exp"), None), check_vma=False
    )
```

time: 50.5 us -> 45.7 us (0.905)
  Pallas kernels: 46 us -> 35.8 us
  local copies, waits for them, and re-layouts: 2.4 us -> 7.93 us
  matrix products: 1.67 us -> 0 us
  other arithmetic: 0.02 us -> 1.44 us
    pallas_call x2, Pallas kernels: 46 us -> 35.8 us  [the longest x1 35.4 us: body(): pl.pallas_call(functools.partial(stack_kernel, sky, exp, capacity), out_s...]
    unnamed x28 -> x15, local copies, waits for them, and re-layouts: 2.09 us -> 7 us
    dot_general x2 -> x0, matrix products: 1.67 us -> none  [toeplitz(): return jnp.einsum('xyk,bk->bxy', picks, basis_vals.astype(jnp.float32))]
    convert_element_type x0 -> x1, other arithmetic: none -> 0.79 us  [body(): cols = jnp.concatenate([basis_cols[:, :1], jnp.zeros((basis_count, 128 -...]
    slice x0 -> x1, local copies, waits for them, and re-layouts: none -> 0.76 us  [body(): basis_cols[:, :0:-1]]
    convert_element_type x1, other arithmetic: 0.01 us -> 0.66 us  [body(): weights.astype(jnp.float32)]
where the time goes in v2:
time: 45.7 us; the launch traced here: 45.2 us
  Pallas kernels  35.8 us (78%)
  local copies, waits for them, and re-layouts  7.93 us (17%)
  other arithmetic  1.44 us (3%)
    pallas_call x1, Pallas kernels, body(): pl.pallas_call(functools.partial(stack_kernel, sky, exp, capacity), out_s...  35.4 us
    unnamed x15, local copies, waits for them, and re-layouts  7 us

profile of v2, /device:TPU:0, one launch (start us, length us, event | category | flops | bytes accessed | tf_op | source)
XLA Modules:
  0.0 45.2 jit_solution(14184565827158415599)
XLA Ops:
  0.0 0.7 %convert_element_type.11.weights = f32[48]{0:T(128)S(1)} convert(bf16[48]{0:T(256)(128)(2,1)} %param.17) | non-fusion elementwise | flops 48 | bytes 288 | tf_op jit(solution)/shard_map/convert_element_type | solution.py:376
  0.7 0.1 pad.6.clone
  0.7 0.8 %slice.7 = bf16[20,40]{1,0:T(8,128)(2,1)S(1)} slice(bf16[20,41]{1,0:T(8,128)(2,1)} %param.21), slice={[0:20], [1:41]} | slice | bytes 3200 | tf_op jit(solution)/shard_map/slice | solution.py:327
  1.5 0.1 rev.3
  1.6 0.8 %maximum_convert_fusion = (f32[20,128]{1,0:T(8,128)S(1)}, f32[20,128]{1,0:T(8,128)S(1)}) fusion(bf16[20,40]{1,0:T(8,128)(2,1)S(1)} %rev.3, bf16[20,1]{1,0:T(8,128)(2,1)} %bitcast.8, bf16[128]{0:T(256)(128)(2,1)S(1)} %pad.6.clone, bf16[20,41]{1,0:T(8,128)(2,1)} %param.20), kind=kLoop, calls=%fused_computation | loop fusion | flops 17920 | bytes 24016 | tf_op jit(solution)/shard_map/convert_element_type | solution.py:330
  2.4 0.9 %copy.12.row_taps = bf16[48,6,24]{2,1,0:T(8,128)(2,1)S(1)} copy(bf16[48,6,24]{0,2,1:T(8,128)(2,1)} %param.13) | data formatting | bytes 27648 | tf_op args[2]
  3.3 0.9 %copy.13.col_taps = bf16[48,6,128]{2,1,0:T(8,128)(2,1)S(1)} copy(bf16[48,6,128]{2,0,1:T(8,128)(2,1)} %param.14) | data formatting | bytes 147456 | tf_op args[3]
  4.2 0.0 copy-start.3
  4.2 0.6 %copy-done.3 = s32[48,1]{0,1:T(1,128)S(1)} copy-done((s32[48,1]{0,1:T(1,128)S(1)}, s32[48,1]{0,1:T(1,128)}, u32[]{:S(2)}) %copy-start.3) | copy-done | bytes 216
  4.8 0.4 plan.1
  5.2 0.0 copy-start
  5.2 1.2 %copy-done = bf16[48,10752]{1,0:T(8,128)(2,1)S(1)} copy-done((bf16[48,10752]{1,0:T(8,128)(2,1)S(1)}, bf16[48,10752]{1,0:T(8,128)(2,1)}, u32[]{:S(2)}) %copy-start) | copy-done | bytes 1032216
  6.4 0.0 copy-start.1
  6.4 0.7 %copy-done.1 = f32[48,20]{0,1:T(8,128)S(1)} copy-done((f32[48,20]{0,1:T(8,128)S(1)}, f32[48,20]{0,1:T(8,128)}, u32[]{:S(2)}) %copy-start.1) | copy-done | bytes 3864
  7.1 0.0 copy-start.2
  7.1 0.7 %copy-done.2 = s32[48,2]{0,1:T(2,128)S(1)} copy-done((s32[48,2]{0,1:T(2,128)S(1)}, s32[48,2]{0,1:T(2,128)}, u32[]{:S(2)}) %copy-start.2) | copy-done | bytes 408
  7.8 0.0 copy-start.4
  7.8 0.7 %copy-done.4 = s32[48]{0:T(128)S(1)} copy-done((s32[48]{0:T(128)S(1)}, s32[48]{0:T(128)}, u32[]{:S(2)}) %copy-start.4) | copy-done | bytes 216
  8.5 0.0 copy-start.5
  8.5 0.7 %copy-done.5 = s32[48]{0:T(128)S(1)} copy-done((s32[48]{0:T(128)S(1)}, s32[48]{0:T(128)}, u32[]{:S(2)}) %copy-start.5) | copy-done | bytes 216
  9.1 35.4 %stack.1 = f32[192,128]{1,0:T(8,128)S(1)} custom-call(bf16[48,10752]{1,0:T(8,128)(2,1)S(1)} %copy-done, f32[20,48]{1,0:T(8,128)S(1)} %bitcast.5, bf16[48,6,24]{2,1,0:T(8,128)(2,1)S(1)} %copy.12.row_taps, bf16[48,6,128]{2,1,0:T(8,128)(2,1)S(1)} %copy.13.col_taps, s32[2,48]{1,0:T(2,128)S(1)} %bitcast.6, s32[48]{0:T(128)S(1)} %copy-done.4, ...), custom_call_target="tpu_custom_call" | custom-call | tf_op jit(solution)/shard_map/stack/pallas_call | solution.py:344
  44.6 0.6 %copy.15 = f32[192,128]{1,0:T(8,128)} copy(f32[192,128]{1,0:T(8,128)S(1)} %stack.1) | data formatting | bytes 196608
  (1 shorter events, 0.0 us)
Async XLA Ops:
  4.2 0.7 %copy-start.3 = (s32[48,1]{0,1:T(1,128)S(1)}, s32[48,1]{0,1:T(1,128)}, u32[]{:S(2)}) copy-start(s32[48,1]{0,1:T(1,128)} %param.18) | copy-start | bytes 580
  5.2 1.2 %copy-start = (bf16[48,10752]{1,0:T(8,128)(2,1)S(1)}, bf16[48,10752]{1,0:T(8,128)(2,1)}, u32[]{:S(2)}) copy-start(bf16[48,10752]{1,0:T(8,128)(2,1)} %tiles.1) | copy-start | bytes 3096580
  6.4 0.7 %copy-start.1 = (f32[48,20]{0,1:T(8,128)S(1)}, f32[48,20]{0,1:T(8,128)}, u32[]{:S(2)}) copy-start(f32[48,20]{0,1:T(8,128)} %param.12) | copy-start | bytes 11524
  7.1 0.7 %copy-start.2 = (s32[48,2]{0,1:T(2,128)S(1)}, s32[48,2]{0,1:T(2,128)}, u32[]{:S(2)}) copy-start(s32[48,2]{0,1:T(2,128)} %param.15) | copy-start | bytes 1156
  7.8 0.7 %copy-start.4 = (s32[48]{0:T(128)S(1)}, s32[48]{0:T(128)}, u32[]{:S(2)}) copy-start(s32[48]{0:T(128)} %words.1) | copy-start | bytes 580
  8.5 0.7 %copy-start.5 = (s32[48]{0:T(128)S(1)}, s32[48]{0:T(128)}, u32[]{:S(2)}) copy-start(s32[48]{0:T(128)} %slots.1) | copy-start | bytes 580

commit v3 on v2

--- a/solution.py
+++ b/solution.py
@@ -11,15 +11,30 @@
 META = 16
 GROUP = 16
 MESH = pl.DeviceIdType.MESH
-VMEM_BYTES = 48 * 1024 * 1024
+VMEM_BYTES = 63 * 1024 * 1024
 
 
 def plan_kernel(
-    sky, capacity, me, dest, rows, cols, plan, row_table, col_table
+    sky,
+    capacity,
+    me,
+    dest,
+    weights,
+    row_taps,
+    col_taps,
+    basis_rows,
+    basis_cols,
+    plan,
+    scale,
+    row_lines,
+    col_lines,
+    row_table,
+    col_table,
+    square,
 ):
     count = dest.shape[1]
-    basis_count = rows.shape[0]
-    tile_rows = row_table.shape[0] // basis_count
+    basis_count, kernel_len = basis_rows.shape
+    taps, tile_rows = row_taps.shape[:2]
     tile_cols = col_table.shape[1]
     lane = lax.broadcasted_iota(jnp.int32, (128, 128), 1)
     line = lax.broadcasted_iota(jnp.int32, (128, 128), 0)
@@ -39,6 +54,21 @@
     plan[...] = jnp.concatenate(
         [order, place, jnp.zeros((6, 128), jnp.float32)], axis=0
     ).astype(jnp.int32)
+    square[...] = jnp.zeros((128, 128), jnp.float32)
+    square[0:1, :count] = weights[...].astype(jnp.float32)
+    scale[...] = square[:8, :]
+    for k in range(taps):
+        square[:tile_rows, :count] = row_taps[k].astype(jnp.float32)
+        row_lines[pl.ds(k, count, stride=8), :] = square[...].T[:count, :]
+        col_lines[pl.ds(k, count, stride=8), :] = col_taps[k].astype(jnp.float32)
+    square[...] = jnp.zeros((128, 128), jnp.float32)
+    square[:basis_count, :kernel_len] = basis_cols[...].astype(jnp.float32)
+    turned = jnp.where(line == (128 - lane) % 128, 1.0, 0.0).astype(jnp.bfloat16)
+    cols = jnp.dot(
+        square[...].astype(jnp.bfloat16), turned, preferred_element_type=jnp.float32
+    )
+    square[:basis_count, :kernel_len] = basis_rows[...].astype(jnp.float32)
+    rows = square[...]
     for b in range(basis_count):
         row = jnp.broadcast_to(rows[b : b + 1, :], (tile_rows, 128))
         row_table[b * tile_rows : (b + 1) * tile_rows, :] = pltpu.roll(
@@ -52,8 +82,7 @@
         )
 
 
-def band(taps, shift, length):
-    count = taps.shape[0]
+def band(taps, count, shift, length):
     width = taps.shape[1]
     source = lax.broadcasted_iota(jnp.int32, (length, width), 0)
     position = lax.broadcasted_iota(jnp.int32, (length, width), 1)
@@ -77,15 +106,17 @@
     sky,
     exp,
     capacity,
+    taps,
+    tile_rows,
     tiles,
     coefs,
-    row_taps,
-    col_taps,
     shifts,
     words,
-    weights,
     slots,
     plan,
+    scale,
+    row_lines,
+    col_lines,
     row_table,
     col_table,
     out,
@@ -115,8 +146,7 @@
         )
     tile_count = tiles.shape[0]
     basis_count = coefs.shape[0]
-    tile_rows = row_taps.shape[2]
-    tile_cols = col_taps.shape[2]
+    tile_cols = col_lines.shape[2]
     in_rows = images.shape[1]
     in_cols = tiles.shape[1] // in_rows
     blocks = tiles.shape[1] // 128
@@ -172,18 +202,18 @@
                 scaled[rows, b * 256 : (b + 1) * 256] = both.astype(jnp.bfloat16)
             return inner
 
-        lax.fori_loop(0, GROUP // 2, pair, 0, unroll=2)
+        lax.fori_loop(0, GROUP // 2, pair, 0, unroll=4)
         matched = jnp.dot(scaled[...], col_table[...], preferred_element_type=jnp.float32)
         for u in range(GROUP):
             t = plan[0, first + u]
             own = matched[u * tile_rows : (u + 1) * tile_rows, :].astype(jnp.bfloat16)
-            row_warp = band(row_taps[t].astype(jnp.float32), shifts[0, t], tile_rows)
-            col_warp = band(col_taps[t].astype(jnp.float32), shifts[1, t], tile_cols)
+            row_warp = band(row_lines[t][:, :tile_rows], taps, shifts[0, t], tile_rows)
+            col_warp = band(col_lines[t], taps, shifts[1, t], tile_cols)
             halfway = lax.dot_general(
                 row_warp, own, (((0,), (0,)), ((), ())), preferred_element_type=jnp.float32
             ).astype(jnp.bfloat16)
             warped = jnp.dot(halfway, col_warp, preferred_element_type=jnp.float32)
-            word, weight = words[t], weights[t]
+            word, weight = words[t], scale[0, t]
             good = jnp.bitwise_and(jnp.right_shift(word, cell), 1) == 0
             prod[first + u] = jnp.where(good, warped * weight, 0.0)
             fine = jnp.bitwise_and(jnp.right_shift(word, jnp.minimum(lane, 31)), 1) == 0
@@ -319,32 +349,36 @@
     chunk = capacity * tile_rows + META
     vmem = pl.BlockSpec(memory_space=pltpu.VMEM)
     smem = pl.BlockSpec(memory_space=pltpu.SMEM)
-    rows = jnp.pad(basis_rows, ((0, 0), (0, 128 - kernel_len))).astype(jnp.float32)
-    cols = jnp.concatenate(
-        [
-            basis_cols[:, :1],
-            jnp.zeros((basis_count, 128 - kernel_len), basis_cols.dtype),
-            basis_cols[:, :0:-1],
-        ],
-        axis=1,
-    ).astype(jnp.float32)
-    plan, row_table, col_table = pl.pallas_call(
+    taps = row_taps.shape[1]
+    plan, scale, row_lines, col_lines, row_table, col_table = pl.pallas_call(
         functools.partial(plan_kernel, sky, capacity),
         out_shape=(
             jax.ShapeDtypeStruct((8, 128), jnp.int32),
+            jax.ShapeDtypeStruct((8, 128), jnp.float32),
+            jax.ShapeDtypeStruct((tile_count * 8, 128), jnp.float32),
+            jax.ShapeDtypeStruct((tile_count * 8, tile_cols), jnp.float32),
             jax.ShapeDtypeStruct((basis_count * tile_rows, 128), jnp.float32),
             jax.ShapeDtypeStruct((basis_count * 256, tile_cols), jnp.bfloat16),
         ),
-        in_specs=[smem, vmem, vmem, vmem],
-        out_specs=(vmem, vmem, vmem),
+        in_specs=[smem] + [vmem] * 6,
+        out_specs=(vmem,) * 6,
+        scratch_shapes=[pltpu.VMEM((128, 128), jnp.float32)],
         compiler_params=pltpu.CompilerParams(vmem_limit_bytes=VMEM_BYTES),
         name="plan",
-    )(lax.axis_index("sky").reshape(1), destination.reshape(1, tile_count), rows, cols)
+    )(
+        lax.axis_index("sky").reshape(1),
+        destination.reshape(1, tile_count),
+        weights.reshape(1, tile_count),
+        row_taps.transpose(1, 2, 0),
+        col_taps.transpose(1, 0, 2),
+        basis_rows,
+        basis_cols,
+    )
     share_rows = SLOTS // exp * tile_rows
     return pl.pallas_call(
-        functools.partial(stack_kernel, sky, exp, capacity),
+        functools.partial(stack_kernel, sky, exp, capacity, taps, tile_rows),
         out_shape=jax.ShapeDtypeStruct((share_rows, tile_cols), jnp.float32),
-        in_specs=[vmem, smem, vmem, vmem, smem, smem, smem, smem, smem, vmem, vmem],
+        in_specs=[vmem] + [smem] * 6 + [vmem] * 4,
         out_specs=vmem,
         scratch_shapes=[
             pltpu.VMEM((GROUP * in_rows, 128), jnp.float32),
@@ -369,13 +403,13 @@
     )(
         padded_tiles,
         coefficients.T,
-        row_taps,
-        col_taps,
         shifts.T,
         mask_words,
-        weights.astype(jnp.float32),
         patch_slot,
         plan,
+        scale,
+        row_lines.reshape(tile_count, 8, 128),
+        col_lines.reshape(tile_count, 8, tile_cols),
         row_table,
         col_table,
     )

time: 45.7 us -> 40.9 us (0.89)
  local copies, waits for them, and re-layouts: 7.93 us -> 1.54 us
  Pallas kernels: 35.8 us -> 39.1 us
  other arithmetic: 1.44 us -> 0 us
    unnamed x15 -> x1, local copies, waits for them, and re-layouts: 7 us -> 1.54 us
    pallas_call x1, Pallas kernels: 0.37 us -> 2.63 us  [body(): pl.pallas_call(functools.partial(plan_kernel, sky, capacity), out_shape=(...]
    convert_element_type x2 -> x0, other arithmetic: 1.44 us -> none  [the longest x1 0.79 us: body(): cols = jnp.concatenate([basis_cols[:, :1], jnp.zeros((basis_count, 128 -...]
    pallas_call x1, Pallas kernels: 35.4 us -> 36.5 us  [body(): pl.pallas_call(functools.partial(stack_kernel, sky, exp, capacity, taps,...]
    slice x1 -> x0, local copies, waits for them, and re-layouts: 0.76 us -> none  [body(): basis_cols[:, :0:-1]]
where the time goes in v3:
time: 40.9 us; the launch traced here: 40.7 us
  Pallas kernels  39.1 us (96%)
  local copies, waits for them, and re-layouts  1.54 us (4%)
    pallas_call x1, Pallas kernels, body(): pl.pallas_call(functools.partial(stack_kernel, sky, exp, capacity, taps,...  36.5 us
    pallas_call x1, Pallas kernels, body(): pl.pallas_call(functools.partial(plan_kernel, sky, capacity), out_shape=(...  2.63 us
    unnamed x1, local copies, waits for them, and re-layouts  1.54 us

profile of v3, /device:TPU:0, one launch (start us, length us, event | category | flops | bytes accessed | tf_op | source)
XLA Modules:
  0.0 40.7 jit_solution(14571310041254620334)
XLA Ops:
  0.0 2.6 %plan.1 = (s32[8,128]{1,0:T(8,128)}, f32[8,128]{1,0:T(8,128)}, f32[384,128]{1,0:T(8,128)}, f32[384,128]{1,0:T(8,128)}, f32[480,128]{1,0:T(8,128)}, /*index=5*/bf16[5120,128]{1,0:T(8,128)(2,1)}) custom-call(s32[1]{0:T(128)} %bitcast.2.me, s32[1,48]{1,0:T(1,128)} %bitcast.15, bf16[1,48]{1,0:T(2,128)(2,1)} %bitcast.16, bf16[6,24,48]{2,1,0:T(8,128)(2,1)} %bitcast.12, ...), custom_call_target="tpu_custom_call" | custom-call | tf_op jit(solution)/shard_map/plan/pallas_call | solution.py:353
  2.6 36.5 %stack.1 = f32[192,128]{1,0:T(8,128)} custom-call(bf16[48,10752]{1,0:T(8,128)(2,1)} %tiles.1, f32[20,48]{1,0:T(8,128)} %bitcast.13, s32[2,48]{1,0:T(2,128)} %bitcast.14, s32[48]{0:T(128)} %words.1, s32[48]{0:T(128)} %slots.1, s32[8,128]{1,0:T(8,128)} %get-tuple-element.11.plan, f32[8,128]{1,0:T(8,128)} %get-tuple-element.12.scale, f32[48,8,128]{2,1,0:T(8,128)} %bitcast.9, ...), custom_call_target="tpu_custom_call" | custom-call | tf_op jit(solution)/shard_map/stack/pallas_call | solution.py:378
  39.1 1.5 %copy.13 = f32[192,128]{1,0:T(8,128)} copy(f32[192,128]{1,0:T(8,128)} %stack.1) | data formatting | bytes 196608
